TPU v7x, 128 devices: a whole 4x4x4 slice. The times are simulated.
128 devices in a mesh: sec: 32 (over z, x, core), col: 4 (over y).
Axes of the slice: x: 4, y: 4, z: 4, core: 2. Of those that a mesh axis runs over, the one named last changes fastest.
Arguments:
- right_sides: float32 [32, 4, 20, 128, 256], P('sec', 'col'), may hold values from -6 to 6
- diag_inverse: float32 [32, 4, 20, 128, 128], P('sec', 'col'), may hold values from -1 to 1
- coupling: float32 [32, 4, 20, 128, 128], P('sec', 'col'), may hold values from -1 to 1
- off_blocks: float32 [32, 4, 15, 16, 128, 128], P('sec', 'col'), may hold values from -0.125 to 0.125
- pattern: int32 [32, 4, 15, 16], P('sec', 'col'), may hold values from 0 to 59, as said below
Outputs:
- solution: float32 [32, 4, 20, 128, 256], P('sec', 'col')
Inputs may be any that keep to these rules, and one draw needn't show every extreme that they name: `pattern`: in a device's list, entry (l - 1) * 5 + k holds 16 different positions below l * 4 * 5, that is of levels under l.
All inputs are finite; a program needn't handle non-finite values.
Results may differ from a plain program's by a relative error of at most 0.0003.
Values sent between devices are 32-bit elements; how exact they have to be, the bound alone decides.
A program may use at most 128 MiB of HBM per device.

v0:
```python
import functools

import jax
import jax.numpy as jnp
from jax import lax
from jax.experimental import pallas as pl
from jax.experimental.pallas import tpu as pltpu
from jax.sharding import PartitionSpec as P

LEV = 4
CHUNKS = 3
SHIFTED = (0, 1, 3)
MESH = pl.DeviceIdType.MESH
F32 = jnp.float32
BF16 = jnp.bfloat16


def split(value):
    high = value.astype(BF16)
    return high, (value - high.astype(F32)).astype(BF16)


def dot(left, right):
    return jnp.dot(left, right, preferred_element_type=F32)


def dot3(left, right):
    left_high, left_low = split(left)
    right_high, right_low = split(right)
    both = dot(left_high, jnp.concatenate([right_high, right_low], axis=1))
    width = right.shape[1]
    return both[:, :width] + both[:, width:] + dot(left_low, right_high)


def dot_ready(left, high, low):
    left_high, left_low = split(left)
    return dot(left_high, high) + dot(left_high, low) + dot(left_low, high)


def section_kernel(
    pattern, right_sides, diag, coupling, off,
    out,
    rhs_v, diag_v, coup_v, off_v, got, table, top,
    z_made, z_here, share, map_cut, map_parts, maps, pairs, groups, lead,
    span_high, span_low, reach_high, reach_low,
    base_cut, base_parts, begun, slices, sums, ends, entered, enter_high, enter_low,
    in_sem, out_sem, send_sem, recv_sem, far_send, far_recv,
):
    me, sec = lax.axis_index("col"), lax.axis_index("sec")
    core = lax.rem(sec, 2)
    x = lax.rem(sec // 2, 4)
    z = sec // 8
    right, left, across = lax.rem(me + 1, 4), lax.rem(me + 3, 4), lax.rem(me + 2, 4)
    boundary = me == 3
    per_level = diag_v.shape[0] // LEV
    bs = diag_v.shape[1]
    items = (LEV - 1) * CHUNKS
    last_row = LEV * per_level - 1
    last_low = (LEV - 1) * per_level - 1
    below = (LEV - 2) * 4 * per_level
    positions = (LEV - 1) * 4 * per_level
    piece = slices.shape[1]

    def start_all(copies):
        for copy in copies:
            copy.start()

    def at(x_step=0, y_step=0, z_step=0, to_core=None):
        there = core if to_core is None else to_core
        return {
            "sec": (lax.rem(z + z_step, 4) * 4 + lax.rem(x + x_step, 4)) * 2 + there,
            "col": lax.rem(me + y_step, 4),
        }

    partners = [dict(x_step=i) for i in (1, 2, 3)] + [dict(z_step=i) for i in (1, 2, 3)]
    partners += [dict(y_step=j) for j in (1, 2, 3)] + [dict(y_step=j, to_core=1 - core) for j in range(4)]

    def level_rows(level):
        return pl.ds(level * per_level, per_level)

    loads = []
    for level in range(LEV):
        rows = level_rows(level)
        parts = [(coupling.at[rows], coup_v.at[rows]), (diag.at[rows], diag_v.at[rows]), (right_sides.at[rows], rhs_v.at[rows])]
        if level:
            lower = level_rows(level - 1)
            parts.append((off.at[lower], off_v.at[lower]))
        loads.append([pltpu.make_async_copy(a, b, in_sem.at[level, i]) for i, (a, b) in enumerate(parts)])
    barrier = pltpu.get_barrier_semaphore()
    for partner in partners:
        pl.semaphore_signal(barrier, inc=1, device_id=at(**partner), device_id_type=MESH)
    start_all(loads[0])


    def count_of(item):
        return 4 if item in SHIFTED else 2

    def ring(item, slot, p, index, target, own_index=None):
        size = per_level * bs // count_of(item)
        ref = got.at[item, slot, pl.ds(p * size, size)]
        return pltpu.make_async_remote_copy(
            src_ref=ref, dst_ref=ref,
            send_sem=send_sem.at[item, index if own_index is None else own_index], recv_sem=recv_sem.at[item, index],
            device_id={"col": target}, device_id_type=MESH,
        )

    def own_sends(item):
        count = count_of(item)
        copies = []
        for p in range(count):
            copies.append(ring(item, me, p, p, right))
            copies.append(ring(item, me, count - 1 - p, 4 + count - 1 - p, left))
        return copies

    def from_left(item, p):
        return ring(item, left, p, p, right)

    def from_right(item, p):
        return ring(item, right, p, 4 + p, right)

    def to_right(item, p):
        return ring(item, left, p, 8 + p, right)

    def to_left(item, p):
        return ring(item, right, p, 8 + p, left, 12 + p)

    def forward_steps(item):
        if count_of(item) == 2:
            return [(0, True, None), (1, False, None)]
        return [
            (0, True, None), (3, False, None),
            (1, True, left != 2), (2, False, right != 0),
            (2, True, left == 0), (1, False, right == 2),
        ]

    def forward(item):
        for p, rightward, allowed in forward_steps(item):
            (from_left if rightward else from_right)(item, p).wait_recv()
            go = (to_right if rightward else to_left)(item, p)
            if allowed is None:
                go.start()
            else:
                pl.when(allowed)(go.start)

    def finish_near(item):
        from_left(item, count_of(item) - 1).wait_recv()
        from_right(item, 0).wait_recv()

    def finish_far(item):
        for p in range(count_of(item)):
            ring(item, across, p, 8 + p, right).wait_recv()

    def finish(item):
        finish_near(item)
        finish_far(item)

    def ring_sends_end(item):
        for copy in own_sends(item):
            copy.wait_send()
        for p, rightward, allowed in forward_steps(item):
            gone = (to_right if rightward else to_left)(item, p)
            if allowed is None:
                gone.wait_send()
            else:
                pl.when(allowed)(gone.wait_send)

    def to_table(level, chunk, sources=range(4)):
        item = level * CHUNKS + chunk
        first = chunk * positions + level * 4 * per_level

        def body(k, carry):
            for source in sources:
                high, low = split(got[item, source, pl.ds(pl.multiple_of(k * bs, bs), bs), :])
                table[first + source * per_level + k, :, :bs] = high
                table[first + source * per_level + k, :, bs:] = low
            return carry

        lax.fori_loop(0, per_level, body, 0)

    def reduced(row, low_row, chunk, limit=None):
        if chunk == 0:
            current = -coup_v[row]
        else:
            current = rhs_v[row, :, (chunk - 1) * bs : chunk * bs]
        if low_row is None:
            return current
        wide = jnp.zeros((bs, 2 * bs), F32)
        narrow = jnp.zeros((bs, bs), F32)
        for begin in range(0, 16, 4):
            pieces = [split(off_v[low_row, j]) for j in range(begin, begin + 4)]
            places = [pattern[low_row, 0, j] for j in range(begin, begin + 4)]
            if limit is None:
                places = [chunk * positions + place for place in places]
            else:
                places = [jnp.where(place < limit, chunk * positions + place, CHUNKS * positions) for place in places]
            picked = jnp.concatenate([table[place] for place in places], axis=0)
            wide += dot(jnp.concatenate([p[0] for p in pieces], axis=1), picked)
            narrow += dot(jnp.concatenate([p[1] for p in pieces], axis=1), picked[:, :bs])
        return current - (wide[:, :bs] + wide[:, bs:] + narrow)

    def compute(level, chunk):
        def body(k, carry):
            row = level * per_level + k
            solved = dot3(diag_v[row], reduced(row, (level - 1) * per_level + k if level else None, chunk))
            if level < LEV - 1:
                got[level * CHUNKS + chunk, me, pl.ds(pl.multiple_of(k * bs, bs), bs), :] = solved
            else:
                top[chunk, pl.ds(pl.multiple_of(k * bs, bs), bs), :] = solved
            return carry

        lax.fori_loop(0, per_level, body, 0)


    def z_copy(owner, k):
        return pltpu.make_async_remote_copy(
            src_ref=z_made.at[owner, k], dst_ref=z_here.at[k], send_sem=far_send.at[0, owner * per_level + k],
            recv_sem=far_recv.at[0, k], device_id=at(y_step=owner + 1), device_id_type=MESH,
        )

    def z_make(begin, end):
        @pl.when(boundary)
        def _():
            def body(step, carry):
                k, owner = begin + step // 4, lax.rem(step, 4)
                place = below + owner * per_level + k
                which, found = jnp.int32(0), jnp.int32(0)
                for j in range(16):
                    same = (pattern[last_low, 0, j] == place).astype(jnp.int32)
                    which, found = which + j * same, found + same
                block = dot3(diag_v[last_row], off_v[last_low, which])
                z_made[owner, k] = jnp.where(found > 0, -block, jnp.zeros_like(block))
                return carry

            lax.fori_loop(0, 4 * (end - begin), body, 0)
            for k in range(begin, end):
                start_all([z_copy(owner, k) for owner in range(3)])
                z_here[k] = z_made[3, k]

    def z_wait():
        @pl.when(jnp.logical_not(boundary))
        def _():
            for k in range(per_level):
                z_copy(0, k).wait_recv()

    def shared(chunk):
        left_side = jnp.concatenate([z_here[k] for k in range(per_level)], axis=1)
        share[...] = dot3(left_side, got[(LEV - 2) * CHUNKS + chunk, me])

        @pl.when(boundary)
        def _():
            share[...] += dot3(diag_v[last_row], reduced(last_row, last_low, chunk, below))

        return share[...].T


    def far(source, target, phase, index, own_index=None, **step):
        return pltpu.make_async_remote_copy(
            src_ref=source, dst_ref=target,
            send_sem=far_send.at[phase, index if own_index is None else own_index], recv_sem=far_recv.at[phase, index],
            device_id=at(**step), device_id_type=MESH,
        )

    def map_of(which):
        return maps[which].reshape(bs, bs)

    rounds = (1, 2, 3)
    other = 1 - core
    map_scatter = [far(map_cut.at[lax.rem(me + j, 4)], map_parts.at[me], 1, j, y_step=j) for j in rounds]
    map_gather = [far(maps.at[core, me], maps.at[core, me], 2, j, y_step=j) for j in rounds]
    map_swap = far(maps.at[core], maps.at[core], 2, 4, to_core=other)
    pair_round = [far(pairs.at[x], pairs.at[x], 3, j, x_step=j) for j in rounds]
    group_round = [far(groups.at[z], groups.at[z], 4, j, z_step=j) for j in rounds]
    base_scatter = [
        [
            far(base_cut.at[h, lax.rem(me + j, 4)], base_parts.at[core, me], 5 + h, j * 2 + core, j, y_step=j, to_core=h)
            for j in range(4)
        ]
        for h in range(2)
    ]
    slice_round = [far(slices.at[x], slices.at[x], 7, j, x_step=j) for j in rounds]
    sum_round = [far(sums.at[z], sums.at[z], 8, j, z_step=j) for j in rounds]
    mine = core * 4 + me
    end_round = [
        far(ends.at[core if s == 0 else other], entered.at[mine], 9, j * 2 + s, y_step=j, to_core=core if s == 0 else other)
        for j in range(4) for s in range(2) if j or s
    ]
    eye = (lax.broadcasted_iota(jnp.int32, (bs, bs), 0) == lax.broadcasted_iota(jnp.int32, (bs, bs), 1)).astype(F32)
    nothing = jnp.zeros((bs, bs), F32)

    def wait_all(copies):
        for copy in copies:
            copy.wait_recv()

    def maps_scatter():
        value = shared(0)
        for q in range(4):
            map_cut[q] = value[q * piece : (q + 1) * piece]
        start_all(map_scatter)
        map_parts[me] = map_cut[me]

    def maps_gather():
        wait_all(map_scatter)
        maps[core, me] = (map_parts[0] + map_parts[1]) + (map_parts[2] + map_parts[3])
        start_all(map_gather)

    def maps_swap():
        wait_all(map_gather)
        map_swap.start()

    def maps_round():
        map_swap.wait_recv()
        pairs[x] = dot3(map_of(0), map_of(1))
        start_all(pair_round)

    def maps_products():
        wait_all(pair_round)
        after = [None, None, pairs[3], eye]
        after[1] = dot3(pairs[2], pairs[3])
        after[0] = dot3(pairs[1], after[1])
        groups[z] = dot3(pairs[0], after[0])
        start_all(group_round)
        inside = [None, None, jnp.where(x == 3, eye, nothing), nothing]
        for i in (1, 0):
            inside[i] = jnp.where(x == i + 1, eye, dot3(pairs[i + 1], inside[i + 1]))
        lead[...] = jnp.where(x == 0, eye, dot3(pairs[0], inside[0]))
        for i in range(4):
            for j, value in enumerate((after[i], inside[i])):
                high, low = split(value)
                span_high[i * bs : (i + 1) * bs, j * bs : (j + 1) * bs] = high
                span_low[i * bs : (i + 1) * bs, j * bs : (j + 1) * bs] = low

    def maps_reach():
        wait_all(group_round)
        inside = [None, None, jnp.where(z == 3, lead[...], nothing), nothing]
        for i in (1, 0):
            inside[i] = jnp.where(z == i + 1, lead[...], dot3(groups[i + 1], inside[i + 1]))
        for i in range(4):
            high, low = split(inside[i])
            reach_high[i * bs : (i + 1) * bs, :] = high
            reach_low[i * bs : (i + 1) * bs, :] = low

    def bases_scatter(chunk):
        h = chunk - 1
        value = shared(chunk)
        for q in range(4):
            base_cut[h, q] = value[q * piece : (q + 1) * piece]
        start_all(base_scatter[h][1:])

        @pl.when(core != h)
        def _():
            base_scatter[h][0].start()

        @pl.when(core == h)
        def _():
            base_parts[core, me] = base_cut[h, me]

    def slices_start():
        for h in range(2):

            @pl.when(core == h)
            def _(h=h):
                for j in range(4):
                    for source in range(2):
                        if j or source != h:
                            far(base_cut.at[h, 0], base_parts.at[source, lax.rem(me + 4 - j, 4)], 5 + h, j * 2 + source, j).wait_recv()

        even = (base_parts[0, 0] + base_parts[0, 1]) + (base_parts[0, 2] + base_parts[0, 3])
        odd = (base_parts[1, 0] + base_parts[1, 1]) + (base_parts[1, 2] + base_parts[1, 3])
        begun[...] = even
        slices[x] = dot3(even, map_of(1)) + odd
        start_all(slice_round)

    def sums_start():
        wait_all(slice_round)
        joined = jnp.concatenate([slices[i] for i in range(4)], axis=1)
        both = dot_ready(joined, span_high[...], span_low[...])
        sums[z] = both[:, :bs]
        start_all(sum_round)
        ends[0] = both[:, bs:]

    def ends_start():
        wait_all(sum_round)
        joined = jnp.concatenate([sums[i] for i in range(4)], axis=1)
        enter = ends[0] + dot_ready(joined, reach_high[...], reach_low[...])
        ends[0] = enter
        ends[1] = begun[...] + dot3(enter, map_of(0))
        entered[mine] = ends[core]
        start_all(end_round)

    def z_sends_end():
        @pl.when(boundary)
        def _():
            for k in range(per_level):
                for owner in range(3):
                    z_copy(owner, k).wait_send()

    def sends_end(copies):
        for copy in copies:
            copy.wait_send()

    def bases_sends_end():
        for h in range(2):
            sends_end(base_scatter[h][1:])

            @pl.when(core != h)
            def _(h=h):
                base_scatter[h][0].wait_send()


    def enter():
        wait_all(end_round)
        for h in range(2):
            value = jnp.concatenate([entered[h * 4 + q] for q in range(4)], axis=0).T
            high, low = split(value)
            enter_high[:, h * bs : (h + 1) * bs] = high
            enter_low[:, h * bs : (h + 1) * bs] = low

    def correct(level):
        if level < LEV - 1:
            parts = [got[level * CHUNKS + chunk, me] for chunk in range(CHUNKS)]
        else:
            parts = [top[chunk] for chunk in range(CHUNKS)]
        change = dot_ready(parts[0], enter_high[...], enter_low[...])
        for h in range(2):
            value = parts[1 + h] + change[:, h * bs : (h + 1) * bs]
            rhs_v[level_rows(level), :, h * bs : (h + 1) * bs] = value.reshape(per_level, bs, bs)
        writes[level].start()

    writes = [pltpu.make_async_copy(rhs_v.at[level_rows(level)], out.at[level_rows(level)], out_sem.at[level]) for level in range(LEV)]

    for copy in loads[0][:2]:
        copy.wait()
    compute(0, 0)
    pl.semaphore_wait(barrier, len(partners))
    start_all(own_sends(0))
    for group in loads[1:]:
        start_all(group)
    loads[0][2].wait()
    compute(0, 1)
    table[CHUNKS * positions] = jnp.zeros((bs, 2 * bs), BF16)
    forward(0)
    start_all(own_sends(1))
    for group in loads[1:]:
        for copy in group:
            copy.wait()
    z_make(0, 2)
    finish(0)
    to_table(0, 0)
    compute(1, 0)
    forward(1)
    start_all(own_sends(3))
    z_make(2, per_level)
    compute(0, 2)
    finish(1)
    to_table(0, 1)
    compute(1, 1)
    forward(3)
    start_all(own_sends(2))
    finish(3)
    to_table(1, 0)
    compute(2, 0)
    z_wait()
    maps_scatter()
    forward(2)
    start_all(own_sends(4))
    finish(2)
    to_table(0, 2)
    compute(1, 2)
    maps_gather()
    forward(4)
    ring_sends_end(0)
    ring_sends_end(1)
    z_sends_end()
    start_all(own_sends(5))
    finish(4)
    to_table(1, 1)
    compute(2, 1)
    bases_scatter(1)
    maps_swap()
    forward(5)
    ring_sends_end(3)
    start_all(own_sends(6))
    maps_round()
    maps_products()
    start_all(own_sends(7))
    finish(5)
    to_table(1, 2)
    compute(2, 2)
    bases_scatter(2)
    forward(6)
    forward(7)
    start_all(own_sends(8))
    ring_sends_end(2)
    ring_sends_end(4)
    sends_end(map_scatter + map_gather + [map_swap] + pair_round + group_round)
    maps_reach()
    slices_start()
    finish(6)
    to_table(2, 0)
    sums_start()
    compute(3, 0)
    ends_start()
    forward(8)
    ring_sends_end(5)
    ring_sends_end(6)
    bases_sends_end()
    sends_end(slice_round)
    finish(7)
    to_table(2, 1)
    compute(3, 1)
    enter()
    for level in range(LEV - 1):
        correct(level)
    finish_near(8)
    to_table(2, 2, (me, left, right))
    finish_far(8)
    to_table(2, 2, (across,))
    compute(3, 2)
    correct(LEV - 1)
    ring_sends_end(7)
    ring_sends_end(8)
    sends_end(sum_round + end_round)
    for copy in writes:
        copy.wait()


def section_solve(right_sides, diag_inverse, coupling, off_blocks, pattern):
    rows, bs, width = right_sides.shape
    per_level = rows // LEV
    items = (LEV - 1) * CHUNKS
    any_space = pl.BlockSpec(memory_space=pl.ANY)
    piece = width // 8
    full = pltpu.VMEM((bs, bs), F32)
    four = pltpu.VMEM((4, bs, bs), F32)
    cut = pltpu.VMEM((4, piece, bs), F32)
    cuts = pltpu.VMEM((2, 4, piece, bs), F32)
    return pl.pallas_call(
        section_kernel,
        out_shape=jax.ShapeDtypeStruct((rows, bs, width), F32),
        in_specs=[pl.BlockSpec(memory_space=pltpu.SMEM)] + [any_space] * 4,
        out_specs=any_space,
        scratch_shapes=[
            pltpu.VMEM((rows, bs, width), F32),
            pltpu.VMEM((rows, bs, bs), F32),
            pltpu.VMEM((rows, bs, bs), F32),
            pltpu.VMEM(off_blocks.shape, F32),
            pltpu.VMEM((items, 4, per_level * bs, bs), F32),
            pltpu.VMEM((CHUNKS * (LEV - 1) * 4 * per_level + 1, bs, 2 * bs), BF16),
            pltpu.VMEM((CHUNKS, per_level * bs, bs), F32),
            pltpu.VMEM((4, per_level, bs, bs), F32),
            pltpu.VMEM((per_level, bs, bs), F32),
            full,
            cut, cut, cuts, four, four, full,
            pltpu.VMEM((4 * bs, 2 * bs), BF16),
            pltpu.VMEM((4 * bs, 2 * bs), BF16),
            pltpu.VMEM((4 * bs, bs), BF16),
            pltpu.VMEM((4 * bs, bs), BF16),
            cuts, cuts,
            pltpu.VMEM((piece, bs), F32),
            cut, cut,
            pltpu.VMEM((2, piece, bs), F32),
            pltpu.VMEM((8, piece, bs), F32),
            pltpu.VMEM((bs, width), BF16),
            pltpu.VMEM((bs, width), BF16),
            pltpu.SemaphoreType.DMA((LEV, 4)),
            pltpu.SemaphoreType.DMA((LEV,)),
            pltpu.SemaphoreType.DMA((items, 16)),
            pltpu.SemaphoreType.DMA((items, 12)),
            pltpu.SemaphoreType.DMA((10, 16)),
            pltpu.SemaphoreType.DMA((10, 16)),
        ],
        compiler_params=pltpu.CompilerParams(collective_id=0, has_side_effects=True, vmem_limit_bytes=58 << 20),
        name="section_solve",
    )(pattern.reshape(pattern.shape[0], 1, pattern.shape[1]), right_sides, diag_inverse, coupling, off_blocks)


def hand_on_kernel(solved, out, held, in_sem, out_sem):
    steps = in_sem.shape[0]
    rows = solved.shape[0] // steps
    loads = [pltpu.make_async_copy(solved.at[pl.ds(i * rows, rows)], held.at[pl.ds(i * rows, rows)], in_sem.at[i]) for i in range(steps)]
    stores = [pltpu.make_async_copy(held.at[pl.ds(i * rows, rows)], out.at[pl.ds(i * rows, rows)], out_sem.at[i]) for i in range(steps)]
    for copy in loads:
        copy.start()
    for load, store in zip(loads, stores):
        load.wait()
        store.start()
    for copy in stores:
        copy.wait()


def hand_on(solved):
    any_space = pl.BlockSpec(memory_space=pl.ANY)
    return pl.pallas_call(
        hand_on_kernel,
        out_shape=jax.ShapeDtypeStruct(solved.shape, F32),
        in_specs=[any_space],
        out_specs=any_space,
        scratch_shapes=[pltpu.VMEM(solved.shape, F32), pltpu.SemaphoreType.DMA((5,)), pltpu.SemaphoreType.DMA((5,))],
        compiler_params=pltpu.CompilerParams(vmem_limit_bytes=58 << 20),
        name="hand_on",
    )(solved)


def per_device(right_sides, diag_inverse, coupling, off_blocks, pattern):
    result = section_solve(right_sides[0, 0], diag_inverse[0, 0], coupling[0, 0], off_blocks[0, 0], pattern[0, 0])
    return hand_on(result)[None, None]


def solution(mesh):
    return jax.shard_map(
        per_device,
        mesh=mesh,
        in_specs=(
            P("sec", "col", None, None, None),
            P("sec", "col", None, None, None),
            P("sec", "col", None, None, None),
            P("sec", "col", None, None, None, None),
            P("sec", "col", None, None),
        ),
        out_specs=P("sec", "col", None, None, None),
        check_vma=False,
    )
```

profile of v0, /device:TPU:0, one launch (start us, length us, event | category | flops | bytes accessed | tf_op | source)
XLA Modules:
  0.0 125.3 jit_solution(17639848029601656371)
XLA Ops:
  0.0 122.7 %section_solve.1.solved = f32[20,128,256]{2,1,0:T(8,128)} custom-call(s32[15,1,16]{2,1,0:T(1,128)} %bitcast.10, f32[20,128,256]{2,1,0:T(8,128)} %bitcast.7, f32[20,128,128]{2,1,0:T(8,128)} %bitcast.8, f32[20,128,128]{2,1,0:T(8,128)} %bitcast.9, f32[15,16,128,128]{3,2,1,0:T(8,128)} %bitcast.6), custom_call_target="tpu_custom_call" | custom-call | tf_op jit(solution)/shard_map/section_solve/pallas_call | solution.py:537
  122.7 2.6 %hand_on.1 = f32[20,128,256]{2,1,0:T(8,128)} custom-call(f32[20,128,256]{2,1,0:T(8,128)} %section_solve.1.solved), custom_call_target="tpu_custom_call" | custom-call | tf_op jit(solution)/shard_map/hand_on/pallas_call | solution.py:593
where the time goes:
time: 127 us; the launch traced here: 125 us
  Pallas kernels  125 us (98%)
    pallas_call x1, Pallas kernels, section_solve(): pl.pallas_call(section_kernel, out_shape=jax.ShapeDtypeStruct((rows, bs,...  123 us
    pallas_call x1, Pallas kernels, hand_on(): pl.pallas_call(hand_on_kernel, out_shape=jax.ShapeDtypeStruct(solved.shap...  2.61 us

commit v1 on v0

--- a/solution.py
+++ b/solution.py
@@ -9,7 +9,7 @@
 
 LEV = 4
 CHUNKS = 3
-SHIFTED = (0, 1, 3)
+SHIFTED = (0, 1, 2, 3)
 MESH = pl.DeviceIdType.MESH
 F32 = jnp.float32
 BF16 = jnp.bfloat16
@@ -482,11 +482,12 @@
     start_all(own_sends(6))
     maps_round()
     maps_products()
-    start_all(own_sends(7))
+    start_all(own_sends(7)[:2])
     finish(5)
     to_table(1, 2)
     compute(2, 2)
     bases_scatter(2)
+    start_all(own_sends(7)[2:])
     forward(6)
     forward(7)
     start_all(own_sends(8))

time: 127 us -> 127 us (level)
  no operation moved by 1% of the time
where the time goes in v1:
time: 127 us; the launch traced here: 126 us
  Pallas kernels  125 us (98%)
    pallas_call x1, Pallas kernels, section_solve(): pl.pallas_call(section_kernel, out_shape=jax.ShapeDtypeStruct((rows, bs,...  123 us
    pallas_call x1, Pallas kernels, hand_on(): pl.pallas_call(hand_on_kernel, out_shape=jax.ShapeDtypeStruct(solved.shap...  2.61 us

profile of v1, /device:TPU:0, one launch (start us, length us, event | category | flops | bytes accessed | tf_op | source)
XLA Modules:
  0.0 125.5 jit_solution(3865248175127388239)
XLA Ops:
  0.0 122.9 %section_solve.1.solved = f32[20,128,256]{2,1,0:T(8,128)} custom-call(s32[15,1,16]{2,1,0:T(1,128)} %bitcast.10, f32[20,128,256]{2,1,0:T(8,128)} %bitcast.7, f32[20,128,128]{2,1,0:T(8,128)} %bitcast.8, f32[20,128,128]{2,1,0:T(8,128)} %bitcast.9, f32[15,16,128,128]{3,2,1,0:T(8,128)} %bitcast.6), custom_call_target="tpu_custom_call" | custom-call | tf_op jit(solution)/shard_map/section_solve/pallas_call | solution.py:538
  122.9 2.6 %hand_on.1 = f32[20,128,256]{2,1,0:T(8,128)} custom-call(f32[20,128,256]{2,1,0:T(8,128)} %section_solve.1.solved), custom_call_target="tpu_custom_call" | custom-call | tf_op jit(solution)/shard_map/hand_on/pallas_call | solution.py:594

commit v2 on v1

--- a/solution.py
+++ b/solution.py
@@ -198,7 +198,7 @@
             narrow += dot(jnp.concatenate([p[1] for p in pieces], axis=1), picked[:, :bs])
         return current - (wide[:, :bs] + wide[:, bs:] + narrow)
 
-    def compute(level, chunk):
+    def compute(level, chunk, start=0, stop=per_level):
         def body(k, carry):
             row = level * per_level + k
             solved = dot3(diag_v[row], reduced(row, (level - 1) * per_level + k if level else None, chunk))
@@ -208,7 +208,7 @@
                 top[chunk, pl.ds(pl.multiple_of(k * bs, bs), bs), :] = solved
             return carry
 
-        lax.fori_loop(0, per_level, body, 0)
+        lax.fori_loop(start, stop, body, 0)
 
 
     def z_copy(owner, k):
@@ -416,17 +416,24 @@
             enter_low[:, h * bs : (h + 1) * bs] = low
 
     def correct(level):
-        if level < LEV - 1:
-            parts = [got[level * CHUNKS + chunk, me] for chunk in range(CHUNKS)]
-        else:
-            parts = [top[chunk] for chunk in range(CHUNKS)]
+        parts = [got[level * CHUNKS + chunk, me] for chunk in range(CHUNKS)]
         change = dot_ready(parts[0], enter_high[...], enter_low[...])
         for h in range(2):
             value = parts[1 + h] + change[:, h * bs : (h + 1) * bs]
             rhs_v[level_rows(level), :, h * bs : (h + 1) * bs] = value.reshape(per_level, bs, bs)
         writes[level].start()
 
-    writes = [pltpu.make_async_copy(rhs_v.at[level_rows(level)], out.at[level_rows(level)], out_sem.at[level]) for level in range(LEV)]
+    def correct_top(h):
+        change = dot_ready(top[0], enter_high[:, h * bs : (h + 1) * bs], enter_low[:, h * bs : (h + 1) * bs])
+        rhs_v[level_rows(LEV - 1), :, h * bs : (h + 1) * bs] = (top[1 + h] + change).reshape(per_level, bs, bs)
+        writes[LEV - 1 + h].start()
+
+    writes = [
+        pltpu.make_async_copy(rhs_v.at[level_rows(level)], out.at[level_rows(level)], out_sem.at[level]) for level in range(LEV - 1)
+    ]
+    for h in range(2):
+        part = (level_rows(LEV - 1), slice(None), pl.ds(h * bs, bs))
+        writes.append(pltpu.make_async_copy(rhs_v.at[part], out.at[part], out_sem.at[LEV - 1 + h]))
 
     for copy in loads[0][:2]:
         copy.wait()
@@ -491,17 +498,18 @@
     forward(6)
     forward(7)
     start_all(own_sends(8))
-    ring_sends_end(2)
-    ring_sends_end(4)
-    sends_end(map_scatter + map_gather + [map_swap] + pair_round + group_round)
     maps_reach()
     slices_start()
     finish(6)
     to_table(2, 0)
+    compute(3, 0, 0, 2)
     sums_start()
-    compute(3, 0)
+    compute(3, 0, 2)
     ends_start()
     forward(8)
+    ring_sends_end(2)
+    ring_sends_end(4)
+    sends_end(map_scatter + map_gather + [map_swap] + pair_round + group_round)
     ring_sends_end(5)
     ring_sends_end(6)
     bases_sends_end()
@@ -512,12 +520,13 @@
     enter()
     for level in range(LEV - 1):
         correct(level)
+    correct_top(0)
     finish_near(8)
     to_table(2, 2, (me, left, right))
     finish_far(8)
     to_table(2, 2, (across,))
     compute(3, 2)
-    correct(LEV - 1)
+    correct_top(1)
     ring_sends_end(7)
     ring_sends_end(8)
     sends_end(sum_round + end_round)
@@ -564,7 +573,7 @@
             pltpu.VMEM((bs, width), BF16),
             pltpu.VMEM((bs, width), BF16),
             pltpu.SemaphoreType.DMA((LEV, 4)),
-            pltpu.SemaphoreType.DMA((LEV,)),
+            pltpu.SemaphoreType.DMA((LEV + 1,)),
             pltpu.SemaphoreType.DMA((items, 16)),
             pltpu.SemaphoreType.DMA((items, 12)),
             pltpu.SemaphoreType.DMA((10, 16)),

time: 127 us -> 127 us (level)
  no operation moved by 1% of the time
where the time goes in v2:
time: 127 us; the launch traced here: 126 us
  Pallas kernels  125 us (98%)
    pallas_call x1, Pallas kernels, section_solve(): pl.pallas_call(section_kernel, out_shape=jax.ShapeDtypeStruct((rows, bs,...  123 us
    pallas_call x1, Pallas kernels, hand_on(): pl.pallas_call(hand_on_kernel, out_shape=jax.ShapeDtypeStruct(solved.shap...  2.61 us

profile of v2, /device:TPU:0, one launch (start us, length us, event | category | flops | bytes accessed | tf_op | source)
XLA Modules:
  0.0 125.6 jit_solution(14406731943872100480)
XLA Ops:
  0.0 122.8 %section_solve.1.solved = f32[20,128,256]{2,1,0:T(8,128)} custom-call(s32[15,1,16]{2,1,0:T(1,128)} %bitcast.10, f32[20,128,256]{2,1,0:T(8,128)} %bitcast.7, f32[20,128,128]{2,1,0:T(8,128)} %bitcast.8, f32[20,128,128]{2,1,0:T(8,128)} %bitcast.9, f32[15,16,128,128]{3,2,1,0:T(8,128)} %bitcast.6), custom_call_target="tpu_custom_call" | custom-call | tf_op jit(solution)/shard_map/section_solve/pallas_call | solution.py:547
  122.8 2.6 %hand_on.1 = f32[20,128,256]{2,1,0:T(8,128)} custom-call(f32[20,128,256]{2,1,0:T(8,128)} %section_solve.1.solved), custom_call_target="tpu_custom_call" | custom-call | tf_op jit(solution)/shard_map/hand_on/pallas_call | solution.py:603
